TPU v7x, 32 devices: a whole 2x2x4 slice. The times are simulated.
32 devices in a mesh: groups: 2 (over y), expert: 4 (over z), dp: 2 (over x), sub: 2 (over core).
Axes of the slice: x: 2, y: 2, z: 4, core: 2. Of those that a mesh axis runs over, the one named last changes fastest.
Arguments:
- tokens: bfloat16 [384, 4096], P(('groups', 'expert', 'dp', 'sub')), parts along dimension 0, may hold values from -6 to 6
- cotangent: bfloat16 [384, 4096], P(('groups', 'expert', 'dp', 'sub')), parts along dimension 0, may hold values from -1.5 to 1.5
- routes: int32 [384, 2], P(('groups', 'expert', 'dp', 'sub')), parts along dimension 0, may hold values from 0 to 3, all different within a row; in each aligned block of 12 rows (0 to 11, 12 to 23, ...) at most 12 rows name the same one
- probs: bfloat16 [384, 2], P(('groups', 'expert', 'dp', 'sub')), parts along dimension 0, may hold values from 0.19921875 to 1
- gate_weight: bfloat16 [4, 1536, 4096], P('expert', ('dp', 'sub')), may hold values from -0.09375 to 0.09375
- up_weight: bfloat16 [4, 1536, 4096], P('expert', ('dp', 'sub')), may hold values from -0.09375 to 0.09375
- down_weight: bfloat16 [4, 1536, 4096], P('expert', ('dp', 'sub')), may hold values from -0.09375 to 0.09375
- keep: int32 [4, 1536], P('expert'), may hold values 0 or 1
Outputs:
- fisher: float32 [8, 1536, 1536], P(('groups', 'expert'), ('dp', 'sub')), parts along dimension 0
- masks: float32 [8, 1536], P(('groups', 'expert'), ('dp', 'sub')), parts along dimension 0
- token_scores: float32 [384, 2], P(('groups', 'expert', 'dp', 'sub')), parts along dimension 0
There are 2 independent parts, one for each index of `groups`. A program takes and returns all parts, laid end to end along the dimension named above; an argument that names none is the same for every part. Nothing has to cross between parts.
Inputs may be any that keep to these rules, and one draw needn't show every extreme that they name: `routes`: the 2 experts of a token differ. Among the tokens of one device (aligned blocks of 12 rows) no expert is named more than 12 times, a bound that some block reaches.
All inputs are finite; a program needn't handle non-finite values. No bound on the sum of `keep` on one device may be relied on, other than what follows from the above.
Results may differ from a plain program's by a relative error of at most 0.0041.
Values may be sent and summed in bfloat16 or wider, within the bound.
A program may use at most 64 MiB of HBM per device.

v0:
```python
import jax
import jax.numpy as jnp
from jax import lax
from jax.sharding import PartitionSpec as P


def make_grads(w_gate, w_up, w_down):

    def compute(shards, first_row):
        rows_tok, rows_cot, rows_prob = shards
        dims = (((1,), (1,)), ((), ()))
        gate_pre = lax.dot_general(w_gate, rows_tok, dims, preferred_element_type=jnp.float32)
        up_pre = lax.dot_general(w_up, rows_tok, dims, preferred_element_type=jnp.float32)
        back_pre = lax.dot_general(w_down, rows_cot, dims, preferred_element_type=jnp.float32)
        scale = rows_prob.astype(jnp.float32)[None, :]
        return (scale * (jax.nn.silu(gate_pre) * up_pre) * back_pre).astype(jnp.bfloat16)

    return compute


def local(tokens, cotangent, routes, probs, gate_weight, up_weight, down_weight, keep):
    experts = lax.axis_size("expert")
    tok_rows, picks = routes.shape
    capacity = max(2, 2 * tok_rows * picks // experts)
    unit_count = gate_weight.shape[1]
    pair_count = tok_rows * picks
    flat_routes = routes.reshape(pair_count)
    onehot = (flat_routes[:, None] == jnp.arange(experts, dtype=jnp.int32)[None, :]).astype(
        jnp.int32
    )
    before = jnp.cumsum(onehot, axis=0) - onehot
    slot_index = jnp.sum(onehot * before, axis=1)
    target = flat_routes * capacity + slot_index
    dispatch_map = (
        jnp.arange(experts * capacity, dtype=jnp.int32)[:, None] == target[None, :]
    ).astype(jnp.float32)
    per_token = jnp.sum(dispatch_map.reshape(experts * capacity, tok_rows, picks), axis=2).astype(
        jnp.bfloat16
    )
    tok_send = jnp.dot(per_token, tokens, preferred_element_type=jnp.float32).astype(jnp.bfloat16)
    cot_send = jnp.dot(per_token, cotangent, preferred_element_type=jnp.float32).astype(
        jnp.bfloat16
    )
    prob_send = jnp.dot(
        dispatch_map, probs.astype(jnp.float32).reshape(pair_count), precision=lax.Precision.HIGHEST
    ).astype(jnp.bfloat16)
    tok_recv, cot_recv, prob_recv = (
        lax.all_to_all(tok_send, "expert", split_axis=0, concat_axis=0, tiled=True),
        lax.all_to_all(cot_send, "expert", split_axis=0, concat_axis=0, tiled=True),
        lax.all_to_all(prob_send, "expert", split_axis=0, concat_axis=0, tiled=True),
    )
    dims = (((1,), (1,)), ((), ()))
    compute = make_grads(gate_weight[0], up_weight[0], down_weight[0])
    grads_mine = compute(
        lax.all_gather((tok_recv, cot_recv, prob_recv), ("dp", "sub"), axis=0, tiled=True),
        jnp.int32(0),
    )
    squares = jnp.sum(jnp.square(grads_mine.astype(jnp.float32)), axis=0)
    owned = lax.psum_scatter(squares, ("dp", "sub"), scatter_dimension=0, tiled=True)
    fisher_rows = lax.dot_general(
        grads_mine,
        lax.all_gather(grads_mine, ("dp", "sub"), axis=0, tiled=True),
        dims,
        preferred_element_type=jnp.float32,
    )
    first_unit = lax.axis_index(("dp", "sub")) * unit_count
    returned = lax.all_to_all(owned, "expert", split_axis=0, concat_axis=0, tiled=True)
    pair_totals = jnp.dot(dispatch_map.T, returned, precision=lax.Precision.HIGHEST)
    token_scores = jnp.sqrt(pair_totals + 1e-05).reshape(tok_rows, picks)
    kept_units = keep[0].astype(jnp.float32)
    pull = jnp.dot(fisher_rows, 1.0 - kept_units, precision=lax.Precision.HIGHEST)
    diag_block = lax.dynamic_slice_in_dim(fisher_rows, first_unit, unit_count, 1)
    diagonal_part = jnp.diagonal(diag_block)
    kept_mine = lax.dynamic_slice_in_dim(kept_units, first_unit, unit_count, 0)
    masks = kept_mine * (1.0 + pull / (diagonal_part + 1e-05))
    return (fisher_rows[None], masks[None], token_scores)


def solution(mesh):
    in_specs = (
        P(("groups", "expert", "dp", "sub"), None),
        P(("groups", "expert", "dp", "sub"), None),
        P(("groups", "expert", "dp", "sub"), None),
        P(("groups", "expert", "dp", "sub"), None),
        P("expert", ("dp", "sub"), None),
        P("expert", ("dp", "sub"), None),
        P("expert", ("dp", "sub"), None),
        P("expert", None),
    )
    out_specs = (
        P(("groups", "expert"), ("dp", "sub"), None),
        P(("groups", "expert"), ("dp", "sub")),
        P(("groups", "expert", "dp", "sub"), None),
    )
    return jax.shard_map(local, mesh=mesh, in_specs=in_specs, out_specs=out_specs, check_vma=False)
```

profile of v0, /device:TPU:0, one launch (start us, length us, event | category | flops | bytes accessed | tf_op | source)
XLA Modules:
  0.0 120.0 jit_solution(12046629007377192870)
XLA Ops:
  7.2 0.9 copy.42
  10.0 1.2 convolution_convert_fusion.1
  11.2 0.9 all_to_all.35
  12.1 20.9 %all_to_all.49 = bf16[4,12,4096]{2,1,0:T(8,128)(2,1)} all-to-all(bf16[4,12,4096]{2,1,0:T(8,128)(2,1)} %all_to_all.35), channel_id=1, replica_groups=mesh['groups'=2,'expert'=4,'dp'=2,'sub'=2] {'expert'}, dimensions={0} | all-to-all | bytes 786432 | tf_op jit(solution)/shard_map/all_to_all | solution.py:48
  33.0 1.9 %all_to_all.37 = bf16[48,4096]{1,0:T(8,128)(2,1)} reshape(bf16[4,12,4096]{2,1,0:T(8,128)(2,1)} %all_to_all.49) | data formatting | bytes 786432 | tf_op jit(solution)/shard_map/all_to_all | solution.py:48
  35.0 1.2 convolution_convert_fusion
  36.2 0.9 all_to_all.38
  37.1 17.8 %all_to_all.50 = bf16[4,12,4096]{2,1,0:T(8,128)(2,1)} all-to-all(bf16[4,12,4096]{2,1,0:T(8,128)(2,1)} %all_to_all.38), channel_id=1, replica_groups=mesh['groups'=2,'expert'=4,'dp'=2,'sub'=2] {'expert'}, dimensions={0} | all-to-all | bytes 786432 | tf_op jit(solution)/shard_map/all_to_all | solution.py:49
  54.9 1.9 %all_to_all.40 = bf16[48,4096]{1,0:T(8,128)(2,1)} reshape(bf16[4,12,4096]{2,1,0:T(8,128)(2,1)} %all_to_all.50) | data formatting | bytes 786432 | tf_op jit(solution)/shard_map/all_to_all | solution.py:49
  56.8 0.7 copy.43
  58.4 0.7 all_to_all.44
  59.1 3.2 %all-to-all-start = ((bf16[4,12,1]{1,2,0:T(2,128)(2,1)}), bf16[4,12,1]{1,2,0:T(2,128)(2,1)S(1)}, u32[]{:S(2)}, u32[]{:S(2)}) async-start(bf16[4,12,1]{1,2,0:T(2,128)(2,1)} %all_to_all.44), calls=%async_computation | async-start | bytes 4096 | tf_op jit(solution)/shard_map/all_to_all | solution.py:50
  62.4 1.3 %fusion.41 = (u32[1]{0:T(128)}, u32[1]{0:T(128)}) fusion(u32[32]{0:T(128)} %constant.59, u32[]{:T(128)S(6)} %add.55, u32[]{:T(128)S(6)} %add.52), kind=kLoop, calls=%fused_computation.46 | loop fusion | bytes 24
  65.0 2.8 %all-to-all-done = bf16[4,12,1]{1,2,0:T(2,128)(2,1)S(1)} async-done(((bf16[4,12,1]{1,2,0:T(2,128)(2,1)}), bf16[4,12,1]{1,2,0:T(2,128)(2,1)S(1)}, u32[]{:S(2)}, u32[]{:S(2)}) %all-to-all-start) | async-done | bytes 128 | tf_op jit(solution)/shard_map/all_to_all | solution.py:50
  68.1 6.1 %all-reduce = bf16[192]{0:T(256)(128)(2,1)S(1)} all-reduce(bf16[192]{0:T(256)(128)(2,1)S(1)} %dynamic-update-slice), channel_id=1, replica_groups=mesh['groups'=2,'expert'=4,'dp'=2,'sub'=2] {'dp','sub'}, use_global_device_ids=true, to_apply=%add | all-reduce | flops 192 | bytes 768
  74.3 3.7 %fusion.6 = f32[384,192]{0,1:T(8,128)S(1)} fusion(bf16[192,4096]{1,0:T(8,128)(2,1)} %all-gather.3.cloned.1.call-done, bf16[1,384,4096]{2,1,0:T(8,128)(2,1)} %param.12), kind=kOutput, calls=%fused_computation.9 | convolution fusion | flops 603979776 | bytes 5013504 | tf_op jit(solution)/shard_map/dot_general | solution.py:12
  78.1 1.2 fusion.15
  79.3 2.7 %multiply_reduce_fusion = (f32[192]{0:T(256)S(1)}, bf16[384,192]{0,1:T(8,128)(2,1)S(1)}) fusion(f32[384,192]{0,1:T(8,128)S(1)} %fusion.15, bf16[192,4096]{1,0:T(8,128)(2,1)} %all-gather.5.cloned.1.call-done, bf16[1,384,4096]{2,1,0:T(8,128)(2,1)S(1)} %copy-done), kind=kOutput, calls=%fused_computation.22 | convolution fusion | flops 604348224 | bytes 5161728 | tf_op jit(solution)/shard_map/dot_general | solution.py:14
  82.0 7.5 %all_gather.15 = bf16[1536,192]{0,1:T(8,128)(2,1)S(1)} all-gather(bf16[384,192]{0,1:T(8,128)(2,1)S(1)} %get-tuple-element.24), channel_id=1, replica_groups=mesh['groups'=2,'expert'=4,'dp'=2,'sub'=2] {'dp','sub'}, dimensions={0}, use_global_device_ids=true | all-gather | bytes 737280 | tf_op jit(solution)/shard_map/all_gather | solution.py:62
  90.0 1.0 constant_dynamic-slice_fusion
  91.6 2.1 %convolution_reduce_fusion = f32[384]{0:T(512)S(1)} fusion(f32[384,1536]{1,0:T(8,128)S(1)} %fusion.42, s32[1,1536]{1,0:T(1,128)S(1)} %copy-done.3), kind=kOutput, calls=%fused_computation.16 | convolution fusion | flops 7080960 | bytes 2366976 | tf_op jit(solution)/shard_map/dot_general | solution.py:71
  93.7 6.3 %all-reduce.1 = f32[192]{0:T(256)S(1)} all-reduce(f32[192]{0:T(256)S(1)} %get-tuple-element.23), channel_id=2, replica_groups=mesh['groups'=2,'expert'=4,'dp'=2,'sub'=2] {'dp','sub'}, use_global_device_ids=true, to_apply=%region_4.5.clone | all-reduce | flops 192 | bytes 1536
  100.7 3.2 %all-to-all-start.3 = ((f32[4,12,1]{1,2,0:T(1,128)}), f32[4,12,1]{1,2,0:T(1,128)S(1)}, u32[]{:S(2)}, u32[]{:S(2)}) async-start(f32[4,12,1]{1,2,0:T(1,128)} %bitcast.9), calls=%async_computation.3 | async-start | bytes 4096 | tf_op jit(solution)/shard_map/all_to_all | solution.py:67
  103.9 6.4 %gather_fusion = f32[384]{0:T(512)S(1)} fusion(f32[384,384]{1,0:T(8,128)} %constant_dynamic-slice_fusion, s32[384]{0:T(512)S(1)} %or_reduce_fusion), kind=kCustom, calls=%fused_computation | custom fusion | bytes 6144 | tf_op jit(solution)/shard_map/jit(diagonal)/cond/branch_0_fun/gather | solution.py:73
  (50 shorter events, 8.0 us)
Async XLA Ops:
  7.2 72.2 %copy-start = (bf16[1,384,4096]{2,1,0:T(8,128)(2,1)S(1)}, bf16[1,384,4096]{2,1,0:T(8,128)(2,1)}, u32[]{:S(2)}) copy-start(bf16[1,384,4096]{2,1,0:T(8,128)(2,1)} %param.14) | copy-start | bytes 9437188
  7.2 67.1 %all-gather.3.cloned.1.call-start = ((), (), s32[]{:S(2)}) async-start(), calls=%async_computation.4 | async-start | bytes 1966080 | tf_op jit(solution)/shard_map/all_gather | solution.py:55
  8.5 0.5 copy-start.4
  34.9 27.4 %copy-start.3 = (s32[1,1536]{1,0:T(1,128)S(1)}, s32[1,1536]{1,0:T(1,128)}, u32[]{:S(2)}) copy-start(s32[1,1536]{1,0:T(1,128)} %param.15) | copy-start | bytes 18436
  34.9 44.4 %all-gather.5.cloned.1.call-start = ((), (), s32[]{:S(2)}) async-start(), calls=%async_computation.5 | async-start | bytes 1966080 | tf_op jit(solution)/shard_map/all_gather | solution.py:55
  59.1 8.7 %all-to-all-start = ((bf16[4,12,1]{1,2,0:T(2,128)(2,1)}), bf16[4,12,1]{1,2,0:T(2,128)(2,1)S(1)}, u32[]{:S(2)}, u32[]{:S(2)}) async-start(bf16[4,12,1]{1,2,0:T(2,128)(2,1)} %all_to_all.44), calls=%async_computation | async-start | bytes 4096 | tf_op jit(solution)/shard_map/all_to_all | solution.py:50
  74.3 3.7 %copy-start.2 = (bf16[192,4096]{1,0:T(8,128)(2,1)S(1)}, bf16[192,4096]{1,0:T(8,128)(2,1)}, u32[]{:S(2)}) copy-start(bf16[192,4096]{1,0:T(8,128)(2,1)} %all-gather.3.cloned.1.call-done) | copy-start | bytes 4718596
  74.3 3.8 %copy-start.5 = (bf16[1,384,4096]{2,1,0:T(8,128)(2,1)S(1)}, bf16[1,384,4096]{2,1,0:T(8,128)(2,1)}, u32[]{:S(2)}) copy-start(bf16[1,384,4096]{2,1,0:T(8,128)(2,1)} %param.13) | copy-start | bytes 9437188
  90.0 1.6 %copy-start.1 = (f32[384,1536]{1,0:T(8,128)}, f32[384,1536]{1,0:T(8,128)S(1)}, u32[]{:S(2)}) copy-start(f32[384,1536]{1,0:T(8,128)S(1)} %fusion.42) | copy-start | bytes 7077892
  100.7 10.2 %all-to-all-start.3 = ((f32[4,12,1]{1,2,0:T(1,128)}), f32[4,12,1]{1,2,0:T(1,128)S(1)}, u32[]{:S(2)}, u32[]{:S(2)}) async-start(f32[4,12,1]{1,2,0:T(1,128)} %bitcast.9), calls=%async_computation.3 | async-start | bytes 4096 | tf_op jit(solution)/shard_map/all_to_all | solution.py:67
Sparse Core Ops, SparseCore 0:
  35.0 18.7 all-gather.2
  56.9 18.8 all-gather.4
where the time goes:
time: 121 us; the launch traced here: 120 us
  blocking collectives  58.7 us (49%)
  local copies, waits for them, and re-layouts  21.2 us (18%)
  between operations  15.5 us (13%)
  matrix products  12.8 us (11%)
  starting transfers between devices  6.4 us (5%)
  waiting for transfers between devices  2.85 us (2%)
  other arithmetic  2.48 us (2%)
    all_to_all x1, blocking collectives, local(): lax.all_to_all(tok_send, 'expert', split_axis=0, concat_axis=0, tiled=True)  20.9 us
    all_to_all x1, blocking collectives, local(): lax.all_to_all(cot_send, 'expert', split_axis=0, concat_axis=0, tiled=True)  17.8 us
    unnamed x2, blocking collectives  12.4 us
    all_gather x1, blocking collectives, local(): lax.all_gather(grads_mine, ('dp', 'sub'), axis=0, tiled=True)  7.49 us
    gather x1, local copies, waits for them, and re-layouts, local(): diagonal_part = jnp.diagonal(diag_block)  6.41 us
    unnamed x19, local copies, waits for them, and re-layouts  5.09 us
    dot_general x1, matrix products, compute(): lax.dot_general(w_gate, rows_tok, dims, preferred_element_type=jnp.float32)  3.71 us
    all_to_all x1, starting transfers between devices, local(): lax.all_to_all(owned, 'expert', split_axis=0, concat_axis=0, tiled=True)  3.16 us
  transfers between devices with their start and end apart: 4, of which 1 were waited for; matrix products, arithmetic and copies ran while one was open for 14% of the time, Pallas kernels for 0%

commit v1 on v0

--- a/solution.py
+++ b/solution.py
@@ -1,7 +1,265 @@
+import functools
+
 import jax
 import jax.numpy as jnp
 from jax import lax
+from jax.experimental import pallas as pl
+from jax.experimental.pallas import tpu as pltpu
 from jax.sharding import PartitionSpec as P
+
+MESH = pl.DeviceIdType.MESH
+SLOT = 16
+LANES = 128
+
+
+def pack(values, front):
+    rows, width = values.shape
+    quarter = width // 4
+    last = values[:, 3 * quarter:]
+    folded = [last[4 * j:4 * j + 4] for j in range(3)] + [jnp.zeros((4, quarter), values.dtype)]
+    lower = jnp.concatenate([jnp.zeros((4, LANES), values.dtype)] * (front is not None) + folded, axis=1)
+    upper = values if front is None else jnp.concatenate([front, values], axis=1)
+    return jnp.concatenate([upper, lower], axis=0)
+
+
+def fused(
+    tokens, cotangent, routes, probs, w_gate, w_up, w_down, keep,
+    fisher, masks, scores,
+    tok, cot, wgu, wd, pre, back, grads, totals, returned,
+    load_sem, tok_send, tok_recv, cot_send, cot_recv, grad_send, grad_recv, tot_send, tot_recv,
+    *, planes,
+):
+    z, x, s = lax.axis_index("expert"), lax.axis_index("dp"), lax.axis_index("sub")
+    units = w_down.shape[1]
+    width = tokens.shape[1]
+    quarter = width // 4
+    count = planes * 4
+
+    loads = [
+        pltpu.make_async_copy(w_gate.at[0], wgu.at[pl.ds(0, units)], load_sem.at[0]),
+        pltpu.make_async_copy(w_up.at[0], wgu.at[pl.ds(units, units)], load_sem.at[1]),
+        pltpu.make_async_copy(w_down.at[0], wd, load_sem.at[2]),
+    ]
+    for load in loads:
+        load.start()
+
+    barrier = pltpu.get_barrier_semaphore()
+    others = [lax.rem(z + k, planes) for k in range(1, planes)]
+    across = 1 - x
+    twin = 1 - s
+    for other in others:
+        pl.semaphore_signal(barrier, inc=1, device_id={"expert": other}, device_id_type=MESH)
+    pl.semaphore_signal(barrier, inc=1, device_id={"dp": across}, device_id_type=MESH)
+    pl.semaphore_signal(barrier, inc=1, device_id={"sub": twin}, device_id_type=MESH)
+
+    def slot(plane, column, core):
+        return (plane * 2 + column) * 2 + core
+
+    mine = slot(z, x, s)
+    picked = routes[...]
+    lane = lax.broadcasted_iota(jnp.int32, (picked.shape[0], LANES), 1)
+    weight = probs[...].astype(jnp.float32)
+    front = jnp.zeros(lane.shape, jnp.float32)
+    for k in range(picked.shape[1]):
+        front = front + jnp.where(lane == picked[:, k:k + 1], weight[:, k:k + 1], 0.0)
+    tok[mine] = pack(tokens[...].astype(jnp.float32), front).astype(jnp.bfloat16)
+    cot[mine] = pack(cotangent[...].astype(jnp.float32), None).astype(jnp.bfloat16)
+
+    pl.semaphore_wait(barrier, planes + 1)
+
+    def sender(buffer, sent, send_sem, recv_sem):
+        def copy(index, number, target):
+            part = buffer.at[index, :, pl.ds(0, sent)]
+            return pltpu.make_async_remote_copy(
+                src_ref=part, dst_ref=part, send_sem=send_sem.at[number], recv_sem=recv_sem.at[index],
+                device_id=target, device_id_type=MESH,
+            )
+        return copy
+
+    tok_copy = sender(tok, LANES + 3 * quarter, tok_send, tok_recv)
+    cot_copy = sender(cot, 3 * quarter, cot_send, cot_recv)
+    pending = []
+
+    def start(copy, index, number, target):
+        one = copy(index, number, target)
+        one.start()
+        pending.append(one)
+
+    def begin(copy):
+        start(copy, mine, 0, {"dp": across})
+        for k, other in enumerate(others):
+            start(copy, mine, 1 + k, {"expert": other})
+        start(copy, mine, planes, {"sub": twin})
+
+    def arrive(copy, index):
+        copy(index, 0, {"sub": twin}).wait_recv()
+
+    def relay(copy):
+        number = planes + 1
+        for k in range(planes):
+            if k > 0:
+                index = slot(others[planes - 1 - k], x, s)
+                arrive(copy, index)
+                start(copy, index, number, {"dp": across})
+                start(copy, index, number + 1, {"sub": twin})
+                number += 2
+        for k in range(planes):
+            index = slot(z if k == 0 else others[planes - 1 - k], across, s)
+            arrive(copy, index)
+            start(copy, index, number, {"sub": twin})
+            number += 1
+
+    def finish(copy):
+        for plane in [z] + others[::-1]:
+            arrive(copy, slot(plane, x, twin))
+            arrive(copy, slot(plane, across, twin))
+
+    def unfold(buffer, base):
+        @pl.loop(0, count)
+        def _(index):
+            folded = buffer[index, :, pl.ds(base, 3 * quarter)].astype(jnp.float32)[12:16]
+            pieces = [folded[:, j * quarter:(j + 1) * quarter] for j in range(3)]
+            whole = jnp.concatenate(pieces + [jnp.zeros((4, quarter), jnp.float32)], axis=0)
+            buffer[index, :, pl.ds(base + 3 * quarter, quarter)] = whole.astype(jnp.bfloat16)
+
+    dims = (((1,), (1,)), ((), ()))
+    begin(tok_copy)
+    begin(cot_copy)
+    relay(tok_copy)
+    finish(tok_copy)
+    relay(cot_copy)
+    unfold(tok, LANES)
+    loads[0].wait()
+    loads[1].wait()
+    step = 2 * units // 3
+
+    @pl.loop(0, 3)
+    def _(part):
+        rows = pl.ds(pl.multiple_of(part * step, step), step)
+        left = tok[:, :, pl.ds(LANES, width)].reshape(count * SLOT, width)
+        pre[part] = lax.dot_general(left, wgu[rows], dims, preferred_element_type=jnp.float32)
+
+    loads[2].wait()
+    finish(cot_copy)
+    unfold(cot, 0)
+
+    back[...] = lax.dot_general(
+        cot[...].reshape(count * SLOT, width), wd[...], dims, preferred_element_type=jnp.float32
+    )
+    both = jnp.concatenate([pre[0], pre[1], pre[2]], axis=1)
+    gate, up = both[:, :units], both[:, units:]
+    front_all = tok[:, :, pl.ds(0, LANES)].reshape(count * SLOT, LANES).astype(jnp.float32)
+    lane_all = lax.broadcasted_iota(jnp.int32, front_all.shape, 1)
+    scale = jnp.sum(jnp.where(lane_all == z, front_all, 0.0), axis=1, keepdims=True)
+    row = lax.rem(lax.broadcasted_iota(jnp.int32, scale.shape, 0), SLOT)
+    scale = jnp.where(row < 12, scale, 0.0)
+    silu = gate / (1.0 + jnp.exp(-gate))
+    value = scale * (silu * up) * back[...]
+    own = x * 2 + s
+    compact = jnp.concatenate([value[SLOT * i:SLOT * i + 12] for i in range(count)], axis=0)
+    grads[own] = compact.astype(jnp.bfloat16)
+
+    def grad_copy(index, number, target):
+        return pltpu.make_async_remote_copy(
+            src_ref=grads.at[index], dst_ref=grads.at[index], send_sem=grad_send.at[number],
+            recv_sem=grad_recv.at[index], device_id=target, device_id_type=MESH,
+        )
+
+    start(grad_copy, own, 0, {"dp": across})
+    start(grad_copy, own, 1, {"sub": twin})
+    far = across * 2 + s
+    arrive(grad_copy, far)
+    start(grad_copy, far, 2, {"sub": twin})
+    arrive(grad_copy, x * 2 + twin)
+    arrive(grad_copy, across * 2 + twin)
+
+    kept = keep[...].astype(jnp.float32)
+    square = jnp.zeros((count * 12, LANES), jnp.float32)
+    pulled = jnp.zeros((count * 12, LANES), jnp.float32)
+    for part in range(4):
+        for tile in range(units // LANES):
+            piece = grads[part, :, pl.ds(tile * LANES, LANES)].astype(jnp.float32)
+            first = part * units + tile * LANES
+            square = square + piece * piece
+            pulled = pulled + piece * (1.0 - kept[:, first:first + LANES])
+    for index in range(count):
+        totals[index] = jnp.concatenate(
+            [square[12 * index:12 * index + 12], jnp.zeros((4, LANES), jnp.float32)], axis=0
+        )
+
+    def total_copy(plane, number, target):
+        return pltpu.make_async_remote_copy(
+            src_ref=totals.at[slot(plane, x, s)], dst_ref=returned.at[z], send_sem=tot_send.at[number],
+            recv_sem=tot_recv.at[z], device_id=target, device_id_type=MESH,
+        )
+
+    for k, other in enumerate(others):
+        start(total_copy, other, k, {"expert": other})
+    returned[z] = totals[mine]
+
+    ours = grads[own]
+    for part in range(4):
+        fisher[0, :, pl.ds(part * units, units)] = lax.dot_general(
+            ours, grads[part], (((0,), (0,)), ((), ())), preferred_element_type=jnp.float32
+        )
+    wide = ours.astype(jnp.float32)
+    pull = jnp.sum(wide * jnp.sum(pulled, axis=1, keepdims=True), axis=0, keepdims=True)
+    diagonal = jnp.sum(wide * wide, axis=0, keepdims=True)
+    kept_mine = jnp.zeros((1, units), jnp.float32)
+    for part in range(4):
+        kept_mine = kept_mine + jnp.where(own == part, kept[:, part * units:(part + 1) * units], 0.0)
+    masks[...] = kept_mine * (1.0 + pull / (diagonal + 1e-05))
+
+    for other in others:
+        pltpu.make_async_remote_copy(
+            src_ref=totals.at[mine], dst_ref=returned.at[other], send_sem=tot_send.at[0],
+            recv_sem=tot_recv.at[other], device_id={"expert": other}, device_id_type=MESH,
+        ).wait_recv()
+    result = jnp.zeros((12, picked.shape[1]), jnp.float32)
+    choice = routes[...]
+    for plane in range(planes):
+        total = jnp.sum(returned[plane], axis=1, keepdims=True)[:12]
+        result = result + jnp.where(choice == plane, total, 0.0)
+    scores[...] = jnp.sqrt(result + 1e-05)
+    for one in pending:
+        one.wait_send()
+
+
+def fused_call(tokens, cotangent, routes, probs, gate_weight, up_weight, down_weight, keep):
+    planes = lax.axis_size("expert")
+    count = planes * 4
+    units, width = gate_weight.shape[1:]
+    dma = pltpu.SemaphoreType.DMA
+    vmem, hbm = pl.BlockSpec(memory_space=pltpu.VMEM), pl.BlockSpec(memory_space=pl.ANY)
+    sends = 3 * planes + 3
+    return pl.pallas_call(
+        functools.partial(fused, planes=planes),
+        out_shape=(
+            jax.ShapeDtypeStruct((1, units, 4 * units), jnp.float32),
+            jax.ShapeDtypeStruct((1, units), jnp.float32),
+            jax.ShapeDtypeStruct(routes.shape, jnp.float32),
+        ),
+        in_specs=[vmem] * 4 + [hbm] * 3 + [vmem],
+        out_specs=(vmem, vmem, vmem),
+        scratch_shapes=[
+            pltpu.VMEM((count, SLOT, LANES + width), jnp.bfloat16),
+            pltpu.VMEM((count, SLOT, width), jnp.bfloat16),
+            pltpu.VMEM((2 * units, width), jnp.bfloat16),
+            pltpu.VMEM((units, width), jnp.bfloat16),
+            pltpu.VMEM((3, count * SLOT, 2 * units // 3), jnp.float32),
+            pltpu.VMEM((count * SLOT, units), jnp.float32),
+            pltpu.VMEM((4, count * 12, units), jnp.bfloat16),
+            pltpu.VMEM((count, SLOT, LANES), jnp.float32),
+            pltpu.VMEM((planes, SLOT, LANES), jnp.float32),
+            dma((3,)), dma((sends + planes,)), dma((count,)), dma((sends + planes,)), dma((count,)),
+            dma((3,)), dma((4,)), dma((planes,)), dma((planes,)),
+        ],
+        compiler_params=pltpu.CompilerParams(
+            collective_id=0, has_side_effects=True, vmem_limit_bytes=48 * 1024 * 1024
+        ),
+        cost_estimate=pl.CostEstimate(flops=2 * 10**9, bytes_accessed=12 * 10**6, transcendentals=10**5),
+        name="fisher_masks",
+    )(tokens, cotangent, routes, probs, gate_weight, up_weight, down_weight, keep)
 
 
 def make_grads(w_gate, w_up, w_down):
@@ -21,6 +279,11 @@
 def local(tokens, cotangent, routes, probs, gate_weight, up_weight, down_weight, keep):
     experts = lax.axis_size("expert")
     tok_rows, picks = routes.shape
+    columns, cores = lax.axis_size("dp"), lax.axis_size("sub")
+    if (experts, columns, cores, tok_rows) == (4, 2, 2, 12):
+        return fused_call(
+            tokens, cotangent, routes, probs, gate_weight, up_weight, down_weight, keep
+        )
     capacity = max(2, 2 * tok_rows * picks // experts)
     unit_count = gate_weight.shape[1]
     pair_count = tok_rows * picks

time: 121 us -> 58.4 us (0.48)
  blocking collectives: 58.7 us -> 0 us
  Pallas kernels: 0 us -> 49 us
  between operations: 15.5 us -> 0.64 us
  matrix products: 12.8 us -> 0 us
  local copies, waits for them, and re-layouts: 21.2 us -> 8.52 us
  starting transfers between devices: 6.4 us -> 0 us
  waiting for transfers between devices: 2.85 us -> 0 us
  other arithmetic: 2.48 us -> 0 us
    pallas_call x0 -> x1, Pallas kernels: none -> 49 us  [fused_call(): pl.pallas_call(functools.partial(fused, planes=planes), out_shape=(jax.Sh...]
    all_to_all x2 -> x0, blocking collectives: 38.8 us -> none  [the longest x1 20.9 us: local(): lax.all_to_all(tok_send, 'expert', split_axis=0, concat_axis=0, tiled=True)]
    dot_general x9 -> x0, matrix products: 12.8 us -> none  [the longest x1 3.71 us: compute(): lax.dot_general(w_gate, rows_tok, dims, preferred_element_type=jnp.float32)]
    unnamed x2 -> x0, blocking collectives: 12.4 us -> none
    all_to_all x9 -> x0, local copies, waits for them, and re-layouts: 7.58 us -> none  [the longest x2 2.76 us: local(): lax.all_to_all(cot_send, 'expert', split_axis=0, concat_axis=0, tiled=True)]
    all_gather x1 -> x0, blocking collectives: 7.49 us -> none  [local(): lax.all_gather(grads_mine, ('dp', 'sub'), axis=0, tiled=True)]
    gather x1 -> x0, local copies, waits for them, and re-layouts: 6.41 us -> none  [local(): diagonal_part = jnp.diagonal(diag_block)]
    all_to_all x2 -> x0, starting transfers between devices: 6.32 us -> none  [the longest x1 3.16 us: local(): lax.all_to_all(owned, 'expert', split_axis=0, concat_axis=0, tiled=True)]
  transfers between devices with their start and end apart: 4 -> 0, of which waited for: 1 -> 0; matrix products, arithmetic and copies ran while one was open for 14% -> 0% of each run, Pallas kernels for 0% -> 0%
where the time goes in v1:
time: 58.4 us; the launch traced here: 58.2 us
  Pallas kernels  49 us (84%)
  local copies, waits for them, and re-layouts  8.52 us (15%)
  between operations  0.64 us (1%)
    pallas_call x1, Pallas kernels, fused_call(): pl.pallas_call(functools.partial(fused, planes=planes), out_shape=(jax.Sh...  49 us
    unnamed x12, local copies, waits for them, and re-layouts  7.88 us

profile of v1, /device:TPU:0, one launch (start us, length us, event | category | flops | bytes accessed | tf_op | source)
XLA Modules:
  0.0 58.2 jit_solution(8224412203525067445)
XLA Ops:
  0.6 0.7 %copy.12.probs = bf16[12,2]{1,0:T(8,128)(2,1)S(1)} copy(bf16[12,2]{0,1:T(2,128)(2,1)} %param.11) | data formatting | bytes 96 | tf_op args[3]
  1.4 0.8 %copy.11.routes = s32[12,2]{1,0:T(8,128)S(1)} copy(s32[12,2]{0,1:T(2,128)} %param.10) | data formatting | bytes 192 | tf_op args[2]
  2.2 0.0 copy-start
  2.2 1.9 %copy-done = bf16[1,384,4096]{2,1,0:T(8,128)(2,1)S(1)} copy-done((bf16[1,384,4096]{2,1,0:T(8,128)(2,1)S(1)}, bf16[1,384,4096]{2,1,0:T(8,128)(2,1)}, u32[]{:S(2)}) %copy-start) | copy-done | bytes 3145752
  4.0 0.0 copy-start.1
  4.0 0.9 %copy-done.1 = bf16[12,4096]{1,0:T(8,128)(2,1)S(1)} copy-done((bf16[12,4096]{1,0:T(8,128)(2,1)S(1)}, bf16[12,4096]{1,0:T(8,128)(2,1)}, u32[]{:S(2)}) %copy-start.1) | copy-done | bytes 98328
  4.9 0.0 copy-start.2
  5.0 0.9 %copy-done.2 = bf16[12,4096]{1,0:T(8,128)(2,1)S(1)} copy-done((bf16[12,4096]{1,0:T(8,128)(2,1)S(1)}, bf16[12,4096]{1,0:T(8,128)(2,1)}, u32[]{:S(2)}) %copy-start.2) | copy-done | bytes 98328
  5.9 0.0 copy-start.3
  5.9 0.7 %copy-done.3 = s32[1,1536]{1,0:T(1,128)S(1)} copy-done((s32[1,1536]{1,0:T(1,128)S(1)}, s32[1,1536]{1,0:T(1,128)}, u32[]{:S(2)}) %copy-start.3) | copy-done | bytes 6168
  6.5 49.0 %fisher_masks.1 = (f32[1,384,1536]{2,1,0:T(8,128)S(1)}, f32[1,384]{1,0:T(1,128)S(1)}, f32[12,2]{1,0:T(8,128)S(1)}) custom-call(bf16[12,4096]{1,0:T(8,128)(2,1)S(1)} %copy-done.1, bf16[12,4096]{1,0:T(8,128)(2,1)S(1)} %copy-done.2, s32[12,2]{1,0:T(8,128)S(1)} %copy.11.routes, bf16[12,2]{1,0:T(8,128)(2,1)S(1)} %copy.12.probs, ...), custom_call_target="tpu_custom_call" | custom-call | flops 2000000000 | bytes 12000000 | tf_op jit(solution)/shard_map/fisher_masks/pallas_call | solution.py:235
  55.6 0.6 %copy.13 = f32[12,2]{0,1:T(2,128)} copy(f32[12,2]{1,0:T(8,128)S(1)} %get-tuple-element.5) | data formatting | bytes 192 | tf_op jit(solution)/shard_map/fisher_masks/pallas_call | solution.py:235
  56.2 1.4 %copy.16 = f32[1,384,1536]{2,1,0:T(8,128)} copy(f32[1,384,1536]{2,1,0:T(8,128)S(1)} %get-tuple-element.9) | data formatting | bytes 4718592
  57.6 0.6 copy.17
Async XLA Ops:
  2.2 1.9 %copy-start = (bf16[1,384,4096]{2,1,0:T(8,128)(2,1)S(1)}, bf16[1,384,4096]{2,1,0:T(8,128)(2,1)}, u32[]{:S(2)}) copy-start(bf16[1,384,4096]{2,1,0:T(8,128)(2,1)} %w_gate.1) | copy-start | bytes 9437188
  4.0 0.9 %copy-start.1 = (bf16[12,4096]{1,0:T(8,128)(2,1)S(1)}, bf16[12,4096]{1,0:T(8,128)(2,1)}, u32[]{:S(2)}) copy-start(bf16[12,4096]{1,0:T(8,128)(2,1)} %tokens.1) | copy-start | bytes 294916
  4.9 0.9 %copy-start.2 = (bf16[12,4096]{1,0:T(8,128)(2,1)S(1)}, bf16[12,4096]{1,0:T(8,128)(2,1)}, u32[]{:S(2)}) copy-start(bf16[12,4096]{1,0:T(8,128)(2,1)} %cotangent.1) | copy-start | bytes 294916
  5.9 0.7 %copy-start.3 = (s32[1,1536]{1,0:T(1,128)S(1)}, s32[1,1536]{1,0:T(1,128)}, u32[]{:S(2)}) copy-start(s32[1,1536]{1,0:T(1,128)} %keep.1) | copy-start | bytes 18436

commit v2 on v0

--- a/solution.py
+++ b/solution.py
@@ -1,7 +1,382 @@
+import functools
+
 import jax
 import jax.numpy as jnp
 from jax import lax
+from jax.experimental import pallas as pl
+from jax.experimental.pallas import tpu as pltpu
 from jax.sharding import PartitionSpec as P
+
+MESH = pl.DeviceIdType.MESH
+SLOT = 16
+LANES = 128
+
+
+def pack(values, front):
+    rows, width = values.shape
+    quarter = width // 4
+    last = values[:, 3 * quarter:]
+    folded = [last[4 * j:4 * j + 4] for j in range(3)] + [jnp.zeros((4, quarter), values.dtype)]
+    lower = jnp.concatenate([jnp.zeros((4, LANES), values.dtype)] * (front is not None) + folded, axis=1)
+    upper = values if front is None else jnp.concatenate([front, values], axis=1)
+    return jnp.concatenate([upper, lower], axis=0)
+
+
+def column_of(line):
+    n = line.shape[1]
+    same = lax.broadcasted_iota(jnp.int32, (n, n), 0) == lax.broadcasted_iota(jnp.int32, (n, n), 1)
+    return jnp.sum(jnp.where(same, line, jnp.zeros_like(line)), axis=1, keepdims=True)
+
+
+def gather_kernel(
+    tokens, cotangent, routes, probs, w_gate, w_up, w_down,
+    grads, returned,
+    own_tok, own_cot, own_routes, own_probs, tok, cot, wgu, wd, pre, totals,
+    load_sem, block_send, block_recv, grad_send, grad_recv, tot_send, tot_recv,
+    *, planes,
+):
+    z, x, s = lax.axis_index("expert"), lax.axis_index("dp"), lax.axis_index("sub")
+    units = w_down.shape[1]
+    width = tokens.shape[1]
+    quarter = width // 4
+    count = planes * 4
+    across, twin = 1 - x, 1 - s
+
+    barrier = pltpu.get_barrier_semaphore()
+    peers = []
+    for k in range(planes):
+        for column in range(2):
+            for core in range(2):
+                if k + column + core > 0:
+                    peers.append((lax.rem(z + k, planes), lax.rem(x + column, 2), lax.rem(s + core, 2)))
+    for plane, column, core in peers:
+        pl.semaphore_signal(
+            barrier, inc=1, device_id={"expert": plane, "dp": column, "sub": core}, device_id_type=MESH
+        )
+
+    small = [
+        pltpu.make_async_copy(tokens, own_tok, load_sem.at[0]),
+        pltpu.make_async_copy(routes, own_routes, load_sem.at[1]),
+        pltpu.make_async_copy(probs, own_probs, load_sem.at[2]),
+        pltpu.make_async_copy(cotangent, own_cot, load_sem.at[3]),
+    ]
+    loads = [
+        pltpu.make_async_copy(w_gate.at[0], wgu.at[pl.ds(0, units)], load_sem.at[4]),
+        pltpu.make_async_copy(w_up.at[0], wgu.at[pl.ds(units, units)], load_sem.at[5]),
+        pltpu.make_async_copy(w_down.at[0], wd, load_sem.at[6]),
+    ]
+    for load in small:
+        load.start()
+    for load in loads:
+        load.start()
+
+    def slot(plane, column, core):
+        return (plane * 2 + column) * 2 + core
+
+    mine = slot(z, x, s)
+    for load in small:
+        load.wait()
+    picks = routes.shape[0]
+    lane = lax.broadcasted_iota(jnp.int32, (routes.shape[1], LANES), 1).astype(jnp.float32)
+    front = jnp.zeros(lane.shape, jnp.float32)
+    for k in range(picks):
+        picked = column_of(own_routes[k:k + 1, :].astype(jnp.float32))
+        weight = column_of(own_probs[...].astype(jnp.float32)[k:k + 1, :])
+        front = front + jnp.where(lane == picked, weight, 0.0)
+    tok[mine] = pack(own_tok[...].astype(jnp.float32), front).astype(jnp.bfloat16)
+    cot[mine] = pack(own_cot[...].astype(jnp.float32), None).astype(jnp.bfloat16)
+
+    pl.semaphore_wait(barrier, len(peers))
+
+    buffers = (tok, cot)
+    sent = (LANES + 3 * quarter, 3 * quarter)
+    base = (LANES, 0)
+
+    def block(a, index, kind, target):
+        part = buffers[a].at[index, :, pl.ds(0, sent[a])]
+        return pltpu.make_async_remote_copy(
+            src_ref=part, dst_ref=part, send_sem=block_send.at[a, kind, index],
+            recv_sem=block_recv.at[a, index], device_id=target, device_id_type=MESH,
+        )
+
+    def inside(plane):
+        return (plane >= 0) & (plane < planes)
+
+    def own_z(a):
+        for kind, step in ((0, 1), (1, -1)):
+            @pl.when(inside(z + step))
+            def _():
+                block(a, mine, kind, {"expert": z + step}).start()
+
+    def to_x(a, index):
+        block(a, index, 2, {"dp": across}).start()
+
+    def to_core(a, index):
+        block(a, index, 3, {"sub": twin}).start()
+
+    def arrive(a, index):
+        block(a, index, 3, {"sub": twin}).wait_recv()
+
+    def unfold(a, index):
+        folded = buffers[a][index, :, pl.ds(base[a], 3 * quarter)].astype(jnp.float32)[12:16]
+        pieces = [folded[:, j * quarter:(j + 1) * quarter] for j in range(3)]
+        whole = jnp.concatenate(pieces + [jnp.zeros((4, quarter), jnp.float32)], axis=0)
+        buffers[a][index, :, pl.ds(base[a] + 3 * quarter, quarter)] = whole.astype(jnp.bfloat16)
+
+    def at_distance(d, body):
+        for sign in ((-1, 1) if d else (1,)):
+            @pl.when(inside(z + sign * d))
+            def _():
+                body(z + sign * d, sign)
+
+    def z_in(a, d):
+        def body(plane, sign):
+            index = slot(plane, x, s)
+            arrive(a, index)
+
+            @pl.when(inside(z - sign))
+            def _():
+                block(a, index, 0, {"expert": z - sign}).start()
+            to_x(a, index)
+            to_core(a, index)
+            unfold(a, index)
+        at_distance(d, body)
+
+    def x_in(a, d):
+        def body(plane, sign):
+            index = slot(plane, across, s)
+            arrive(a, index)
+            to_core(a, index)
+            unfold(a, index)
+        at_distance(d, body)
+
+    def core_in(a, d):
+        def body(plane, sign):
+            for column in (x, across):
+                index = slot(plane, column, twin)
+                arrive(a, index)
+                unfold(a, index)
+        at_distance(d, body)
+
+    dims = (((1,), (1,)), ((), ()))
+    step = 2 * units // 3
+
+    def project(part):
+        left = tok[:, :, pl.ds(LANES, width)].reshape(count * SLOT, width)
+        pre[part] = lax.dot_general(
+            left, wgu[pl.ds(part * step, step)], dims, preferred_element_type=jnp.float32
+        )
+
+    own_z(0)
+    to_x(0, mine)
+    to_core(0, mine)
+    own_z(1)
+    to_x(1, mine)
+    to_core(1, mine)
+    z_in(0, 1)
+    x_in(0, 0)
+    z_in(1, 1)
+    x_in(1, 0)
+    z_in(0, 2)
+    x_in(0, 1)
+    core_in(0, 0)
+    z_in(1, 2)
+    x_in(1, 1)
+    core_in(1, 0)
+    z_in(0, 3)
+    x_in(0, 2)
+    core_in(0, 1)
+    z_in(1, 3)
+    x_in(1, 2)
+    core_in(1, 1)
+    x_in(0, 3)
+    core_in(0, 2)
+    loads[0].wait()
+    loads[1].wait()
+    core_in(0, 3)
+    project(0)
+    x_in(1, 3)
+    core_in(1, 2)
+    project(1)
+    project(2)
+    loads[2].wait()
+    core_in(1, 3)
+
+    back = lax.dot_general(
+        cot[...].reshape(count * SLOT, width), wd[...], dims, preferred_element_type=jnp.float32
+    )
+    both = jnp.concatenate([pre[0], pre[1], pre[2]], axis=1)
+    gate, up = both[:, :units], both[:, units:]
+    front_all = tok[:, :, pl.ds(0, LANES)].reshape(count * SLOT, LANES).astype(jnp.float32)
+    lane_all = lax.broadcasted_iota(jnp.int32, front_all.shape, 1)
+    scale = jnp.sum(jnp.where(lane_all == z, front_all, 0.0), axis=1, keepdims=True)
+    row = lax.rem(lax.broadcasted_iota(jnp.int32, scale.shape, 0), SLOT)
+    scale = jnp.where(row < 12, scale, 0.0)
+    silu = gate / (1.0 + jnp.exp(-gate))
+    value = scale * (silu * up) * back
+    own = x * 2 + s
+    compact = jnp.concatenate([value[SLOT * i:SLOT * i + 12] for i in range(count)], axis=0)
+    grads[own] = compact.astype(jnp.bfloat16)
+
+    def grad_copy(index, number, target):
+        return pltpu.make_async_remote_copy(
+            src_ref=grads.at[index], dst_ref=grads.at[index], send_sem=grad_send.at[number],
+            recv_sem=grad_recv.at[index], device_id=target, device_id_type=MESH,
+        )
+
+    far = across * 2 + s
+    grad_sends = [
+        grad_copy(own, 0, {"dp": across}), grad_copy(own, 1, {"sub": twin}), grad_copy(far, 2, {"sub": twin})
+    ]
+    grad_sends[0].start()
+    grad_sends[1].start()
+
+    rounded = value.astype(jnp.bfloat16).astype(jnp.float32)
+    square = jnp.zeros((count * SLOT, LANES), jnp.float32)
+    for tile in range(units // LANES):
+        piece = rounded[:, tile * LANES:(tile + 1) * LANES]
+        square = square + piece * piece
+    totals[...] = square.reshape(count, SLOT, LANES)
+    total_sends = []
+    for number, (plane, column, core) in enumerate(peers):
+        copy = pltpu.make_async_remote_copy(
+            src_ref=totals.at[slot(plane, column, core)], dst_ref=returned.at[mine],
+            send_sem=tot_send.at[number], recv_sem=tot_recv.at[mine],
+            device_id={"expert": plane, "dp": column, "sub": core}, device_id_type=MESH,
+        )
+        copy.start()
+        total_sends.append(copy)
+    returned[mine] = totals[mine]
+
+    grad_copy(far, 0, {"sub": twin}).wait_recv()
+    grad_sends[2].start()
+
+    for a in range(2):
+        for kind, step_z in ((0, 1), (1, -1)):
+            @pl.when(inside(z + step_z))
+            def _():
+                block(a, mine, kind, {"expert": z + step_z}).wait_send()
+        for d in range(1, planes):
+            def relayed(plane, sign):
+                @pl.when(inside(z - sign))
+                def _():
+                    block(a, slot(plane, x, s), 0, {"expert": z - sign}).wait_send()
+            at_distance(d, relayed)
+        for plane in range(planes):
+            block(a, slot(plane, x, s), 2, {"dp": across}).wait_send()
+            block(a, slot(plane, x, s), 3, {"sub": twin}).wait_send()
+            block(a, slot(plane, across, s), 3, {"sub": twin}).wait_send()
+    for plane, column, core in peers:
+        index = slot(plane, column, core)
+        pltpu.make_async_remote_copy(
+            src_ref=totals.at[mine], dst_ref=returned.at[index], send_sem=tot_send.at[0],
+            recv_sem=tot_recv.at[index], device_id={"sub": twin}, device_id_type=MESH,
+        ).wait_recv()
+    for copy in total_sends:
+        copy.wait_send()
+    grad_copy(x * 2 + twin, 0, {"sub": twin}).wait_recv()
+    grad_copy(across * 2 + twin, 0, {"sub": twin}).wait_recv()
+    for copy in grad_sends:
+        copy.wait_send()
+
+
+def fisher_kernel(grads, returned, routes, keep, fisher, masks, scores, held, sems, *, planes):
+    own = lax.axis_index("dp") * 2 + lax.axis_index("sub")
+    parts, rows, units = grads.shape
+    ours = grads[own]
+    flipped = ours.T
+    copies = []
+    for part in range(parts):
+        held[part] = jnp.dot(flipped, grads[part], preferred_element_type=jnp.float32)
+        copy = pltpu.make_async_copy(
+            held.at[part], fisher.at[0, :, pl.ds(part * units, units)], sems.at[part]
+        )
+        copy.start()
+        copies.append(copy)
+
+    kept = keep[...].astype(jnp.float32)
+    pulled = jnp.zeros((rows, LANES), jnp.float32)
+    for part in range(parts):
+        for tile in range(units // LANES):
+            first = part * units + tile * LANES
+            piece = grads[part, :, pl.ds(tile * LANES, LANES)].astype(jnp.float32)
+            pulled = pulled + piece * (1.0 - kept[:, first:first + LANES])
+    wide = ours.astype(jnp.float32)
+    pull = jnp.sum(wide * jnp.sum(pulled, axis=1, keepdims=True), axis=0, keepdims=True)
+    diagonal = jnp.sum(wide * wide, axis=0, keepdims=True)
+    kept_mine = jnp.zeros((1, units), jnp.float32)
+    for part in range(parts):
+        kept_mine = kept_mine + jnp.where(own == part, kept[:, part * units:(part + 1) * units], 0.0)
+    masks[...] = kept_mine * (1.0 + pull / (diagonal + 1e-05))
+
+    choice = routes[...]
+    picks, tok_rows = choice.shape
+    same = (
+        lax.broadcasted_iota(jnp.int32, (tok_rows, tok_rows), 0)
+        == lax.broadcasted_iota(jnp.int32, (tok_rows, tok_rows), 1)
+    )
+    result = jnp.zeros(choice.shape, jnp.float32)
+    for plane in range(planes):
+        merged = returned[4 * plane] + returned[4 * plane + 1] + returned[4 * plane + 2] + returned[4 * plane + 3]
+        total = jnp.sum(merged, axis=1, keepdims=True)[:tok_rows]
+        line = jnp.sum(jnp.where(same, total, 0.0), axis=0, keepdims=True)
+        result = result + jnp.where(choice == plane, line, 0.0)
+    scores[...] = jnp.sqrt(result + 1e-05)
+    for copy in copies:
+        copy.wait()
+
+
+def fused(tokens, cotangent, routes, probs, gate_weight, up_weight, down_weight, keep):
+    planes = lax.axis_size("expert")
+    count = planes * 4
+    units, width = gate_weight.shape[1:]
+    tok_rows, picks = routes.shape
+    dma = pltpu.SemaphoreType.DMA
+    vmem, hbm = pl.BlockSpec(memory_space=pltpu.VMEM), pl.BlockSpec(memory_space=pl.ANY)
+    routes, probs = routes.T, probs.T
+    grads, returned = pl.pallas_call(
+        functools.partial(gather_kernel, planes=planes),
+        out_shape=(
+            jax.ShapeDtypeStruct((4, count * 12, units), jnp.bfloat16),
+            jax.ShapeDtypeStruct((count, SLOT, LANES), jnp.float32),
+        ),
+        in_specs=[hbm] * 7,
+        out_specs=(vmem, vmem),
+        scratch_shapes=[
+            pltpu.VMEM((tok_rows, width), jnp.bfloat16),
+            pltpu.VMEM((tok_rows, width), jnp.bfloat16),
+            pltpu.VMEM((picks, tok_rows), jnp.int32),
+            pltpu.VMEM((picks, tok_rows), jnp.bfloat16),
+            pltpu.VMEM((count, SLOT, LANES + width), jnp.bfloat16),
+            pltpu.VMEM((count, SLOT, width), jnp.bfloat16),
+            pltpu.VMEM((2 * units, width), jnp.bfloat16),
+            pltpu.VMEM((units, width), jnp.bfloat16),
+            pltpu.VMEM((3, count * SLOT, 2 * units // 3), jnp.float32),
+            pltpu.VMEM((count, SLOT, LANES), jnp.float32),
+            dma((7,)), dma((2, 4, count)), dma((2, count)),
+            dma((3,)), dma((4,)), dma((count,)), dma((count,)),
+        ],
+        compiler_params=pltpu.CompilerParams(
+            collective_id=0, has_side_effects=True, vmem_limit_bytes=48 * 1024 * 1024
+        ),
+        cost_estimate=pl.CostEstimate(flops=2 * 10**9, bytes_accessed=12 * 10**6, transcendentals=10**5),
+        name="gather_grads",
+    )(tokens, cotangent, routes, probs, gate_weight, up_weight, down_weight)
+    fisher, masks, scores = pl.pallas_call(
+        functools.partial(fisher_kernel, planes=planes),
+        out_shape=(
+            jax.ShapeDtypeStruct((1, units, 4 * units), jnp.float32),
+            jax.ShapeDtypeStruct((1, units), jnp.float32),
+            jax.ShapeDtypeStruct(routes.shape, jnp.float32),
+        ),
+        in_specs=[vmem] * 4,
+        out_specs=(hbm, vmem, vmem),
+        scratch_shapes=[pltpu.VMEM((4, units, units), jnp.float32), dma((4,))],
+        compiler_params=pltpu.CompilerParams(vmem_limit_bytes=16 * 1024 * 1024),
+        cost_estimate=pl.CostEstimate(flops=3 * 10**8, bytes_accessed=3 * 10**6, transcendentals=10**3),
+        name="fisher_masks",
+    )(grads, returned, routes, keep)
+    return fisher, masks, scores.T
 
 
 def make_grads(w_gate, w_up, w_down):
@@ -21,6 +396,9 @@
 def local(tokens, cotangent, routes, probs, gate_weight, up_weight, down_weight, keep):
     experts = lax.axis_size("expert")
     tok_rows, picks = routes.shape
+    columns, cores = lax.axis_size("dp"), lax.axis_size("sub")
+    if (experts, columns, cores, tok_rows) == (4, 2, 2, 12):
+        return fused(tokens, cotangent, routes, probs, gate_weight, up_weight, down_weight, keep)
     capacity = max(2, 2 * tok_rows * picks // experts)
     unit_count = gate_weight.shape[1]
     pair_count = tok_rows * picks

time: 121 us -> 46 us (0.38)
  blocking collectives: 58.7 us -> 0 us
  Pallas kernels: 0 us -> 40.1 us
  local copies, waits for them, and re-layouts: 21.2 us -> 5.03 us
  between operations: 15.5 us -> 0.66 us
  matrix products: 12.8 us -> 0 us
  starting transfers between devices: 6.4 us -> 0 us
  waiting for transfers between devices: 2.85 us -> 0 us
  other arithmetic: 2.48 us -> 0 us
    pallas_call x0 -> x2, Pallas kernels: none -> 40.1 us  [the longest x1 37.8 us: fused(): pl.pallas_call(functools.partial(gather_kernel, planes=planes), out_shape...]
    all_to_all x2 -> x0, blocking collectives: 38.8 us -> none  [the longest x1 20.9 us: local(): lax.all_to_all(tok_send, 'expert', split_axis=0, concat_axis=0, tiled=True)]
    dot_general x9 -> x0, matrix products: 12.8 us -> none  [the longest x1 3.71 us: compute(): lax.dot_general(w_gate, rows_tok, dims, preferred_element_type=jnp.float32)]
    unnamed x2 -> x0, blocking collectives: 12.4 us -> none
    all_to_all x9 -> x0, local copies, waits for them, and re-layouts: 7.58 us -> none  [the longest x2 2.76 us: local(): lax.all_to_all(cot_send, 'expert', split_axis=0, concat_axis=0, tiled=True)]
    all_gather x1 -> x0, blocking collectives: 7.49 us -> none  [local(): lax.all_gather(grads_mine, ('dp', 'sub'), axis=0, tiled=True)]
    gather x1 -> x0, local copies, waits for them, and re-layouts: 6.41 us -> none  [local(): diagonal_part = jnp.diagonal(diag_block)]
    all_to_all x2 -> x0, starting transfers between devices: 6.32 us -> none  [the longest x1 3.16 us: local(): lax.all_to_all(owned, 'expert', split_axis=0, concat_axis=0, tiled=True)]
  transfers between devices with their start and end apart: 4 -> 0, of which waited for: 1 -> 0; matrix products, arithmetic and copies ran while one was open for 14% -> 0% of each run, Pallas kernels for 0% -> 0%
where the time goes in v2:
time: 46 us; the launch traced here: 45.7 us
  Pallas kernels  40.1 us (87%)
  local copies, waits for them, and re-layouts  5.03 us (11%)
  between operations  0.66 us (1%)
    pallas_call x1, Pallas kernels, fused(): pl.pallas_call(functools.partial(gather_kernel, planes=planes), out_shape...  37.8 us
    unnamed x12, local copies, waits for them, and re-layouts  5.03 us
    pallas_call x1, Pallas kernels, fused(): pl.pallas_call(functools.partial(fisher_kernel, planes=planes), out_shape...  2.3 us

profile of v2, /device:TPU:0, one launch (start us, length us, event | category | flops | bytes accessed | tf_op | source)
XLA Modules:
  0.0 45.7 jit_solution(13832969879247920812)
XLA Ops:
  0.6 0.0 copy-start
  0.6 1.9 %copy-done = bf16[1,384,4096]{2,1,0:T(8,128)(2,1)S(1)} copy-done((bf16[1,384,4096]{2,1,0:T(8,128)(2,1)S(1)}, bf16[1,384,4096]{2,1,0:T(8,128)(2,1)}, u32[]{:S(2)}) %copy-start) | copy-done | bytes 3145752
  2.5 0.0 copy-start.1
  2.5 0.9 %copy-done.1 = bf16[12,4096]{1,0:T(8,128)(2,1)S(1)} copy-done((bf16[12,4096]{1,0:T(8,128)(2,1)S(1)}, bf16[12,4096]{1,0:T(8,128)(2,1)}, u32[]{:S(2)}) %copy-start.1) | copy-done | bytes 98328
  3.4 0.0 copy-start.2
  3.4 0.9 %copy-done.2 = bf16[12,4096]{1,0:T(8,128)(2,1)S(1)} copy-done((bf16[12,4096]{1,0:T(8,128)(2,1)S(1)}, bf16[12,4096]{1,0:T(8,128)(2,1)}, u32[]{:S(2)}) %copy-start.2) | copy-done | bytes 98328
  4.3 0.0 copy-start.3
  4.3 0.7 %copy-done.3 = s32[12,2]{0,1:T(2,128)S(1)} copy-done((s32[12,2]{0,1:T(2,128)S(1)}, s32[12,2]{0,1:T(2,128)}, u32[]{:S(2)}) %copy-start.3) | copy-done | bytes 120
  5.0 0.0 copy-start.4
  5.0 0.7 %copy-done.4 = bf16[12,2]{0,1:T(2,128)(2,1)S(1)} copy-done((bf16[12,2]{0,1:T(2,128)(2,1)S(1)}, bf16[12,2]{0,1:T(2,128)(2,1)}, u32[]{:S(2)}) %copy-start.4) | copy-done | bytes 72
  5.7 0.0 copy-start.5
  5.7 37.8 %gather_grads.1 = (bf16[4,192,384]{2,1,0:T(8,128)(2,1)S(1)}, f32[16,16,128]{2,1,0:T(8,128)S(1)}) custom-call(bf16[12,4096]{1,0:T(8,128)(2,1)S(1)} %copy-done.1, bf16[12,4096]{1,0:T(8,128)(2,1)S(1)} %copy-done.2, s32[2,12]{1,0:T(2,128)S(1)} %bitcast.3, bf16[2,12]{1,0:T(2,128)(2,1)S(1)} %bitcast.5, bf16[1,384,4096]{2,1,0:T(8,128)(2,1)S(1)} %copy-done, ...), custom_call_target="tpu_custom_call" | custom-call | flops 2000000000 | bytes 12000000 | tf_op jit(solution)/shard_map/gather_grads/pallas_call | solution.py:337
  43.4 0.0 copy-done.5
  43.4 2.3 %fisher_masks.1 = (f32[1,384,1536]{2,1,0:T(8,128)}, f32[1,384]{1,0:T(1,128)}, f32[2,12]{1,0:T(2,128)}) custom-call(bf16[4,192,384]{2,1,0:T(8,128)(2,1)S(1)} %get-tuple-element.8.grads, f32[16,16,128]{2,1,0:T(8,128)S(1)} %get-tuple-element.9.returned, s32[2,12]{1,0:T(2,128)S(1)} %bitcast.4, s32[1,1536]{1,0:T(1,128)S(1)} %copy-done.5), custom_call_target="tpu_custom_call" | custom-call | flops 300000000 | bytes 3000000 | tf_op jit(solution)/shard_map/fisher_masks/pallas_call | solution.py:365
Async XLA Ops:
  0.6 1.9 %copy-start = (bf16[1,384,4096]{2,1,0:T(8,128)(2,1)S(1)}, bf16[1,384,4096]{2,1,0:T(8,128)(2,1)}, u32[]{:S(2)}) copy-start(bf16[1,384,4096]{2,1,0:T(8,128)(2,1)} %w_gate.1) | copy-start | bytes 9437188
  2.5 0.9 %copy-start.1 = (bf16[12,4096]{1,0:T(8,128)(2,1)S(1)}, bf16[12,4096]{1,0:T(8,128)(2,1)}, u32[]{:S(2)}) copy-start(bf16[12,4096]{1,0:T(8,128)(2,1)} %tokens.1) | copy-start | bytes 294916
  3.4 0.9 %copy-start.2 = (bf16[12,4096]{1,0:T(8,128)(2,1)S(1)}, bf16[12,4096]{1,0:T(8,128)(2,1)}, u32[]{:S(2)}) copy-start(bf16[12,4096]{1,0:T(8,128)(2,1)} %cotangent.1) | copy-start | bytes 294916
  4.3 0.7 %copy-start.3 = (s32[12,2]{0,1:T(2,128)S(1)}, s32[12,2]{0,1:T(2,128)}, u32[]{:S(2)}) copy-start(s32[12,2]{0,1:T(2,128)} %param.10) | copy-start | bytes 292
  5.0 0.7 %copy-start.4 = (bf16[12,2]{0,1:T(2,128)(2,1)S(1)}, bf16[12,2]{0,1:T(2,128)(2,1)}, u32[]{:S(2)}) copy-start(bf16[12,2]{0,1:T(2,128)(2,1)} %param.11) | copy-start | bytes 148
  5.7 37.8 %copy-start.5 = (s32[1,1536]{1,0:T(1,128)S(1)}, s32[1,1536]{1,0:T(1,128)}, u32[]{:S(2)}) copy-start(s32[1,1536]{1,0:T(1,128)} %keep.1) | copy-start | bytes 18436

commit v3 on v2

--- a/solution.py
+++ b/solution.py
@@ -95,7 +95,7 @@
     def block(a, index, kind, target):
         part = buffers[a].at[index, :, pl.ds(0, sent[a])]
         return pltpu.make_async_remote_copy(
-            src_ref=part, dst_ref=part, send_sem=block_send.at[a, kind, index],
+            src_ref=part, dst_ref=part, send_sem=block_send.at[a, kind],
             recv_sem=block_recv.at[a, index], device_id=target, device_id_type=MESH,
         )
 
@@ -103,19 +103,19 @@
         return (plane >= 0) & (plane < planes)
 
     def own_z(a):
-        for kind, step in ((0, 1), (1, -1)):
+        for step in (1, -1):
             @pl.when(inside(z + step))
             def _():
-                block(a, mine, kind, {"expert": z + step}).start()
+                block(a, mine, 0, {"expert": z + step}).start()
 
     def to_x(a, index):
-        block(a, index, 2, {"dp": across}).start()
+        block(a, index, 1, {"dp": across}).start()
 
     def to_core(a, index):
-        block(a, index, 3, {"sub": twin}).start()
+        block(a, index, 2, {"sub": twin}).start()
 
     def arrive(a, index):
-        block(a, index, 3, {"sub": twin}).wait_recv()
+        block(a, index, 2, {"sub": twin}).wait_recv()
 
     def unfold(a, index):
         folded = buffers[a][index, :, pl.ds(base[a], 3 * quarter)].astype(jnp.float32)[12:16]
@@ -237,43 +237,42 @@
         piece = rounded[:, tile * LANES:(tile + 1) * LANES]
         square = square + piece * piece
     totals[...] = square.reshape(count, SLOT, LANES)
-    total_sends = []
-    for number, (plane, column, core) in enumerate(peers):
-        copy = pltpu.make_async_remote_copy(
+    for plane, column, core in peers:
+        pltpu.make_async_remote_copy(
             src_ref=totals.at[slot(plane, column, core)], dst_ref=returned.at[mine],
-            send_sem=tot_send.at[number], recv_sem=tot_recv.at[mine],
+            send_sem=tot_send, recv_sem=tot_recv,
             device_id={"expert": plane, "dp": column, "sub": core}, device_id_type=MESH,
-        )
-        copy.start()
-        total_sends.append(copy)
+        ).start()
     returned[mine] = totals[mine]
 
     grad_copy(far, 0, {"sub": twin}).wait_recv()
     grad_sends[2].start()
 
+    def sent_all(a, kind, blocks):
+        part = buffers[a].at[pl.ds(0, blocks), :, pl.ds(0, sent[a])]
+        pltpu.make_async_remote_copy(
+            src_ref=part, dst_ref=part, send_sem=block_send.at[a, kind],
+            recv_sem=block_recv.at[a, 0], device_id={"sub": twin}, device_id_type=MESH,
+        ).wait_send()
+
+    edge = (z == 0) | (z == planes - 1)
     for a in range(2):
-        for kind, step_z in ((0, 1), (1, -1)):
-            @pl.when(inside(z + step_z))
-            def _():
-                block(a, mine, kind, {"expert": z + step_z}).wait_send()
-        for d in range(1, planes):
-            def relayed(plane, sign):
-                @pl.when(inside(z - sign))
-                def _():
-                    block(a, slot(plane, x, s), 0, {"expert": z - sign}).wait_send()
-            at_distance(d, relayed)
-        for plane in range(planes):
-            block(a, slot(plane, x, s), 2, {"dp": across}).wait_send()
-            block(a, slot(plane, x, s), 3, {"sub": twin}).wait_send()
-            block(a, slot(plane, across, s), 3, {"sub": twin}).wait_send()
-    for plane, column, core in peers:
-        index = slot(plane, column, core)
-        pltpu.make_async_remote_copy(
-            src_ref=totals.at[mine], dst_ref=returned.at[index], send_sem=tot_send.at[0],
-            recv_sem=tot_recv.at[index], device_id={"sub": twin}, device_id_type=MESH,
-        ).wait_recv()
-    for copy in total_sends:
-        copy.wait_send()
+        @pl.when(edge)
+        def _():
+            sent_all(a, 0, 1)
+
+        @pl.when(jnp.logical_not(edge))
+        def _():
+            sent_all(a, 0, planes + 1)
+        sent_all(a, 1, planes)
+        sent_all(a, 2, 2 * planes)
+    others = len(peers)
+    every = pltpu.make_async_remote_copy(
+        src_ref=totals.at[pl.ds(0, others)], dst_ref=returned.at[pl.ds(0, others)],
+        send_sem=tot_send, recv_sem=tot_recv, device_id={"sub": twin}, device_id_type=MESH,
+    )
+    every.wait_recv()
+    every.wait_send()
     grad_copy(x * 2 + twin, 0, {"sub": twin}).wait_recv()
     grad_copy(across * 2 + twin, 0, {"sub": twin}).wait_recv()
     for copy in grad_sends:
@@ -337,8 +336,8 @@
     grads, returned = pl.pallas_call(
         functools.partial(gather_kernel, planes=planes),
         out_shape=(
-            jax.ShapeDtypeStruct((4, count * 12, units), jnp.bfloat16),
-            jax.ShapeDtypeStruct((count, SLOT, LANES), jnp.float32),
+            pltpu.VMEM((4, count * 12, units), jnp.bfloat16),
+            pltpu.VMEM((count, SLOT, LANES), jnp.float32),
         ),
         in_specs=[hbm] * 7,
         out_specs=(vmem, vmem),
@@ -353,11 +352,11 @@
             pltpu.VMEM((units, width), jnp.bfloat16),
             pltpu.VMEM((3, count * SLOT, 2 * units // 3), jnp.float32),
             pltpu.VMEM((count, SLOT, LANES), jnp.float32),
-            dma((7,)), dma((2, 4, count)), dma((2, count)),
-            dma((3,)), dma((4,)), dma((count,)), dma((count,)),
+            dma((7,)), dma((2, 3)), dma((2, count)),
+            dma((3,)), dma((4,)), dma, dma,
         ],
         compiler_params=pltpu.CompilerParams(
-            collective_id=0, has_side_effects=True, vmem_limit_bytes=48 * 1024 * 1024
+            collective_id=0, has_side_effects=True, vmem_limit_bytes=60 * 1024 * 1024
         ),
         cost_estimate=pl.CostEstimate(flops=2 * 10**9, bytes_accessed=12 * 10**6, transcendentals=10**5),
         name="gather_grads",

time: 46 us -> 39.7 us (0.86)
  local copies, waits for them, and re-layouts: 5.03 us -> 0.01 us
  Pallas kernels: 40.1 us -> 38.9 us
    unnamed x12 -> x4, local copies, waits for them, and re-layouts: 5.03 us -> 0.01 us
    pallas_call x1, Pallas kernels: 37.8 us -> 36.6 us  [fused(): pl.pallas_call(functools.partial(gather_kernel, planes=planes), out_shape...]
where the time goes in v3:
time: 39.7 us; the launch traced here: 39.6 us
  Pallas kernels  38.9 us (98%)
  between operations  0.67 us (2%)
    pallas_call x1, Pallas kernels, fused(): pl.pallas_call(functools.partial(gather_kernel, planes=planes), out_shape...  36.6 us
    pallas_call x1, Pallas kernels, fused(): pl.pallas_call(functools.partial(fisher_kernel, planes=planes), out_shape...  2.3 us

profile of v3, /device:TPU:0, one launch (start us, length us, event | category | flops | bytes accessed | tf_op | source)
XLA Modules:
  0.0 39.6 jit_solution(716859288447636414)
XLA Ops:
  0.6 0.0 copy-start
  0.6 0.0 copy-start.1
  0.7 36.6 %gather_grads.1 = (bf16[4,192,384]{2,1,0:T(8,128)(2,1)S(1)}, f32[16,16,128]{2,1,0:T(8,128)S(1)}) custom-call(bf16[12,4096]{1,0:T(8,128)(2,1)} %tokens.1, bf16[12,4096]{1,0:T(8,128)(2,1)} %cotangent.1, s32[2,12]{1,0:T(2,128)} %bitcast.3, bf16[2,12]{1,0:T(2,128)(2,1)} %bitcast.5, bf16[1,384,4096]{2,1,0:T(8,128)(2,1)} %w_gate.1, bf16[1,384,4096]{2,1,0:T(8,128)(2,1)} %w_up.1, ...), custom_call_target="tpu_custom_call" | custom-call | flops 2000000000 | bytes 12000000 | tf_op jit(solution)/shard_map/gather_grads/pallas_call | solution.py:336
  37.2 0.0 copy-done
  37.3 0.0 copy-done.1
  37.3 2.3 %fisher_masks.1 = (f32[1,384,1536]{2,1,0:T(8,128)}, f32[1,384]{1,0:T(1,128)}, f32[2,12]{1,0:T(2,128)}) custom-call(bf16[4,192,384]{2,1,0:T(8,128)(2,1)S(1)} %get-tuple-element.8.grads, f32[16,16,128]{2,1,0:T(8,128)S(1)} %get-tuple-element.9.returned, s32[2,12]{1,0:T(2,128)S(1)} %bitcast.4, s32[1,1536]{1,0:T(1,128)S(1)} %copy-done.1), custom_call_target="tpu_custom_call" | custom-call | flops 300000000 | bytes 3000000 | tf_op jit(solution)/shard_map/fisher_masks/pallas_call | solution.py:364
Async XLA Ops:
  0.6 36.6 %copy-start = (s32[12,2]{0,1:T(2,128)S(1)}, s32[12,2]{0,1:T(2,128)}, u32[]{:S(2)}) copy-start(s32[12,2]{0,1:T(2,128)} %param.10) | copy-start | bytes 292
  0.6 36.6 %copy-start.1 = (s32[1,1536]{1,0:T(1,128)S(1)}, s32[1,1536]{1,0:T(1,128)}, u32[]{:S(2)}) copy-start(s32[1,1536]{1,0:T(1,128)} %keep.1) | copy-start | bytes 18436

commit v4 on v3

--- a/solution.py
+++ b/solution.py
@@ -194,11 +194,11 @@
     loads[0].wait()
     loads[1].wait()
     core_in(0, 3)
+    x_in(1, 3)
     project(0)
-    x_in(1, 3)
-    core_in(1, 2)
     project(1)
     project(2)
+    core_in(1, 2)
     loads[2].wait()
     core_in(1, 3)
 
@@ -212,31 +212,45 @@
     scale = jnp.sum(jnp.where(lane_all == z, front_all, 0.0), axis=1, keepdims=True)
     row = lax.rem(lax.broadcasted_iota(jnp.int32, scale.shape, 0), SLOT)
     scale = jnp.where(row < 12, scale, 0.0)
-    silu = gate / (1.0 + jnp.exp(-gate))
-    value = scale * (silu * up) * back
     own = x * 2 + s
-    compact = jnp.concatenate([value[SLOT * i:SLOT * i + 12] for i in range(count)], axis=0)
-    grads[own] = compact.astype(jnp.bfloat16)
-
-    def grad_copy(index, number, target):
+    far = across * 2 + s
+    half = count * 6
+
+    def grad_copy(index, piece, number, target):
+        part = grads.at[index, pl.ds(piece * half, half)]
         return pltpu.make_async_remote_copy(
-            src_ref=grads.at[index], dst_ref=grads.at[index], send_sem=grad_send.at[number],
-            recv_sem=grad_recv.at[index], device_id=target, device_id_type=MESH,
+            src_ref=part, dst_ref=part, send_sem=grad_send.at[piece, number],
+            recv_sem=grad_recv.at[piece, index], device_id=target, device_id_type=MESH,
         )
 
-    far = across * 2 + s
-    grad_sends = [
-        grad_copy(own, 0, {"dp": across}), grad_copy(own, 1, {"sub": twin}), grad_copy(far, 2, {"sub": twin})
-    ]
-    grad_sends[0].start()
-    grad_sends[1].start()
-
-    rounded = value.astype(jnp.bfloat16).astype(jnp.float32)
+    grad_sends = []
+
+    def grad_start(index, piece, number, target):
+        copy = grad_copy(index, piece, number, target)
+        copy.start()
+        grad_sends.append(copy)
+
+    halves = []
+    for piece in range(2):
+        rows = slice(piece * count * SLOT // 2, (piece + 1) * count * SLOT // 2)
+        silu = gate[rows] / (1.0 + jnp.exp(-gate[rows]))
+        value = scale[rows] * (silu * up[rows]) * back[rows]
+        compact = jnp.concatenate([value[SLOT * i:SLOT * i + 12] for i in range(count // 2)], axis=0)
+        grads[own, pl.ds(piece * half, half)] = compact.astype(jnp.bfloat16)
+        grad_start(own, piece, 0, {"dp": across})
+        grad_start(own, piece, 1, {"sub": twin})
+        halves.append(value)
+
+    rounded = jnp.concatenate(halves, axis=0).astype(jnp.bfloat16).astype(jnp.float32)
     square = jnp.zeros((count * SLOT, LANES), jnp.float32)
     for tile in range(units // LANES):
         piece = rounded[:, tile * LANES:(tile + 1) * LANES]
         square = square + piece * piece
-    totals[...] = square.reshape(count, SLOT, LANES)
+    spread = jnp.where(
+        lane_all == lax.rem(lax.broadcasted_iota(jnp.int32, square.shape, 0), SLOT),
+        jnp.sum(square, axis=1, keepdims=True), 0.0,
+    )
+    totals[...] = jnp.sum(spread.reshape(count, SLOT, LANES), axis=1, keepdims=True)
     for plane, column, core in peers:
         pltpu.make_async_remote_copy(
             src_ref=totals.at[slot(plane, column, core)], dst_ref=returned.at[mine],
@@ -245,8 +259,9 @@
         ).start()
     returned[mine] = totals[mine]
 
-    grad_copy(far, 0, {"sub": twin}).wait_recv()
-    grad_sends[2].start()
+    for piece in range(2):
+        grad_copy(far, piece, 0, {"sub": twin}).wait_recv()
+        grad_start(far, piece, 2, {"sub": twin})
 
     def sent_all(a, kind, blocks):
         part = buffers[a].at[pl.ds(0, blocks), :, pl.ds(0, sent[a])]
@@ -273,8 +288,9 @@
     )
     every.wait_recv()
     every.wait_send()
-    grad_copy(x * 2 + twin, 0, {"sub": twin}).wait_recv()
-    grad_copy(across * 2 + twin, 0, {"sub": twin}).wait_recv()
+    for piece in range(2):
+        grad_copy(x * 2 + twin, piece, 0, {"sub": twin}).wait_recv()
+        grad_copy(across * 2 + twin, piece, 0, {"sub": twin}).wait_recv()
     for copy in grad_sends:
         copy.wait_send()
 
@@ -310,16 +326,12 @@
 
     choice = routes[...]
     picks, tok_rows = choice.shape
-    same = (
-        lax.broadcasted_iota(jnp.int32, (tok_rows, tok_rows), 0)
-        == lax.broadcasted_iota(jnp.int32, (tok_rows, tok_rows), 1)
-    )
     result = jnp.zeros(choice.shape, jnp.float32)
     for plane in range(planes):
-        merged = returned[4 * plane] + returned[4 * plane + 1] + returned[4 * plane + 2] + returned[4 * plane + 3]
-        total = jnp.sum(merged, axis=1, keepdims=True)[:tok_rows]
-        line = jnp.sum(jnp.where(same, total, 0.0), axis=0, keepdims=True)
-        result = result + jnp.where(choice == plane, line, 0.0)
+        line = returned[4 * plane]
+        for part in range(1, 4):
+            line = line + returned[4 * plane + part]
+        result = result + jnp.where(choice == plane, line[:, :tok_rows], 0.0)
     scores[...] = jnp.sqrt(result + 1e-05)
     for copy in copies:
         copy.wait()
@@ -337,7 +349,7 @@
         functools.partial(gather_kernel, planes=planes),
         out_shape=(
             pltpu.VMEM((4, count * 12, units), jnp.bfloat16),
-            pltpu.VMEM((count, SLOT, LANES), jnp.float32),
+            pltpu.VMEM((count, 1, LANES), jnp.float32),
         ),
         in_specs=[hbm] * 7,
         out_specs=(vmem, vmem),
@@ -351,9 +363,9 @@
             pltpu.VMEM((2 * units, width), jnp.bfloat16),
             pltpu.VMEM((units, width), jnp.bfloat16),
             pltpu.VMEM((3, count * SLOT, 2 * units // 3), jnp.float32),
-            pltpu.VMEM((count, SLOT, LANES), jnp.float32),
+            pltpu.VMEM((count, 1, LANES), jnp.float32),
             dma((7,)), dma((2, 3)), dma((2, count)),
-            dma((3,)), dma((4,)), dma, dma,
+            dma((2, 3)), dma((2, 4)), dma, dma,
         ],
         compiler_params=pltpu.CompilerParams(
             collective_id=0, has_side_effects=True, vmem_limit_bytes=60 * 1024 * 1024

time: 39.7 us -> 38.3 us (0.965)
  Pallas kernels: 38.9 us -> 37.5 us
    pallas_call x1, Pallas kernels: 36.6 us -> 35.2 us  [fused(): pl.pallas_call(functools.partial(gather_kernel, planes=planes), out_shape...]
where the time goes in v4:
time: 38.3 us; the launch traced here: 38.2 us
  Pallas kernels  37.5 us (98%)
  between operations  0.67 us (2%)
    pallas_call x1, Pallas kernels, fused(): pl.pallas_call(functools.partial(gather_kernel, planes=planes), out_shape...  35.2 us
    pallas_call x1, Pallas kernels, fused(): pl.pallas_call(functools.partial(fisher_kernel, planes=planes), out_shape...  2.3 us

profile of v4, /device:TPU:0, one launch (start us, length us, event | category | flops | bytes accessed | tf_op | source)
XLA Modules:
  0.0 38.2 jit_solution(9252250053325489326)
XLA Ops:
  0.6 0.0 copy-start
  0.6 0.0 copy-start.1
  0.7 35.2 %gather_grads.1 = (bf16[4,192,384]{2,1,0:T(8,128)(2,1)S(1)}, f32[16,1,128]{2,1,0:T(1,128)S(1)}) custom-call(bf16[12,4096]{1,0:T(8,128)(2,1)} %tokens.1, bf16[12,4096]{1,0:T(8,128)(2,1)} %cotangent.1, s32[2,12]{1,0:T(2,128)} %bitcast.3, bf16[2,12]{1,0:T(2,128)(2,1)} %bitcast.5, bf16[1,384,4096]{2,1,0:T(8,128)(2,1)} %w_gate.1, bf16[1,384,4096]{2,1,0:T(8,128)(2,1)} %w_up.1, ...), custom_call_target="tpu_custom_call" | custom-call | flops 2000000000 | bytes 12000000 | tf_op jit(solution)/shard_map/gather_grads/pallas_call | solution.py:348
  35.9 0.0 copy-done
  35.9 0.0 copy-done.1
  35.9 2.3 %fisher_masks.1 = (f32[1,384,1536]{2,1,0:T(8,128)}, f32[1,384]{1,0:T(1,128)}, f32[2,12]{1,0:T(2,128)}) custom-call(bf16[4,192,384]{2,1,0:T(8,128)(2,1)S(1)} %get-tuple-element.8.grads, f32[16,1,128]{2,1,0:T(1,128)S(1)} %get-tuple-element.9.returned, s32[2,12]{1,0:T(2,128)S(1)} %bitcast.4, s32[1,1536]{1,0:T(1,128)S(1)} %copy-done.1), custom_call_target="tpu_custom_call" | custom-call | flops 300000000 | bytes 3000000 | tf_op jit(solution)/shard_map/fisher_masks/pallas_call | solution.py:376
Async XLA Ops:
  0.6 35.2 %copy-start = (s32[12,2]{0,1:T(2,128)S(1)}, s32[12,2]{0,1:T(2,128)}, u32[]{:S(2)}) copy-start(s32[12,2]{0,1:T(2,128)} %param.10) | copy-start | bytes 292
  0.6 35.2 %copy-start.1 = (s32[1,1536]{1,0:T(1,128)S(1)}, s32[1,1536]{1,0:T(1,128)}, u32[]{:S(2)}) copy-start(s32[1,1536]{1,0:T(1,128)} %keep.1) | copy-start | bytes 18436

commit v5 on v4

--- a/solution.py
+++ b/solution.py
@@ -12,27 +12,18 @@
 LANES = 128
 
 
-def pack(values, front):
-    rows, width = values.shape
-    quarter = width // 4
+def pack(values):
+    quarter = values.shape[1] // 4
     last = values[:, 3 * quarter:]
     folded = [last[4 * j:4 * j + 4] for j in range(3)] + [jnp.zeros((4, quarter), values.dtype)]
-    lower = jnp.concatenate([jnp.zeros((4, LANES), values.dtype)] * (front is not None) + folded, axis=1)
-    upper = values if front is None else jnp.concatenate([front, values], axis=1)
-    return jnp.concatenate([upper, lower], axis=0)
-
-
-def column_of(line):
-    n = line.shape[1]
-    same = lax.broadcasted_iota(jnp.int32, (n, n), 0) == lax.broadcasted_iota(jnp.int32, (n, n), 1)
-    return jnp.sum(jnp.where(same, line, jnp.zeros_like(line)), axis=1, keepdims=True)
+    return jnp.concatenate([values, jnp.concatenate(folded, axis=1)], axis=0)
 
 
 def gather_kernel(
     tokens, cotangent, routes, probs, w_gate, w_up, w_down,
     grads, returned,
-    own_tok, own_cot, own_routes, own_probs, tok, cot, wgu, wd, pre, totals,
-    load_sem, block_send, block_recv, grad_send, grad_recv, tot_send, tot_recv,
+    own_tok, own_cot, own_routes, own_probs, tok, cot, wgu, wd, pre, totals, told, heard,
+    load_sem, block_send, block_recv, grad_send, grad_recv, tot_send, tot_recv, prob_send, prob_recv,
     *, planes,
 ):
     z, x, s = lax.axis_index("expert"), lax.axis_index("dp"), lax.axis_index("sub")
@@ -76,21 +67,19 @@
     mine = slot(z, x, s)
     for load in small:
         load.wait()
-    picks = routes.shape[0]
-    lane = lax.broadcasted_iota(jnp.int32, (routes.shape[1], LANES), 1).astype(jnp.float32)
-    front = jnp.zeros(lane.shape, jnp.float32)
-    for k in range(picks):
-        picked = column_of(own_routes[k:k + 1, :].astype(jnp.float32))
-        weight = column_of(own_probs[...].astype(jnp.float32)[k:k + 1, :])
-        front = front + jnp.where(lane == picked, weight, 0.0)
-    tok[mine] = pack(own_tok[...].astype(jnp.float32), front).astype(jnp.bfloat16)
-    cot[mine] = pack(own_cot[...].astype(jnp.float32), None).astype(jnp.bfloat16)
+    chosen, weight = own_routes[...], own_probs[...].astype(jnp.float32)
+    blank = jnp.zeros((1, LANES - chosen.shape[1]), jnp.float32)
+    for plane in range(planes):
+        line = jnp.sum(jnp.where(chosen == plane, weight, 0.0), axis=0, keepdims=True)
+        told[plane] = jnp.concatenate([line, blank], axis=1)
+    tok[mine] = pack(own_tok[...].astype(jnp.float32)).astype(jnp.bfloat16)
+    cot[mine] = pack(own_cot[...].astype(jnp.float32)).astype(jnp.bfloat16)
 
     pl.semaphore_wait(barrier, len(peers))
 
     buffers = (tok, cot)
-    sent = (LANES + 3 * quarter, 3 * quarter)
-    base = (LANES, 0)
+    sent = (3 * quarter, 3 * quarter)
+    base = (0, 0)
 
     def block(a, index, kind, target):
         part = buffers[a].at[index, :, pl.ds(0, sent[a])]
@@ -162,7 +151,7 @@
     step = 2 * units // 3
 
     def project(part):
-        left = tok[:, :, pl.ds(LANES, width)].reshape(count * SLOT, width)
+        left = tok[...].reshape(count * SLOT, width)
         pre[part] = lax.dot_general(
             left, wgu[pl.ds(part * step, step)], dims, preferred_element_type=jnp.float32
         )
@@ -173,6 +162,12 @@
     own_z(1)
     to_x(1, mine)
     to_core(1, mine)
+    for plane, column, core in peers:
+        pltpu.make_async_remote_copy(
+            src_ref=told.at[plane], dst_ref=heard.at[mine], send_sem=prob_send, recv_sem=prob_recv,
+            device_id={"expert": plane, "dp": column, "sub": core}, device_id_type=MESH,
+        ).start()
+    heard[mine] = told[z]
     z_in(0, 1)
     x_in(0, 0)
     z_in(1, 1)
@@ -200,6 +195,13 @@
     project(2)
     core_in(1, 2)
     loads[2].wait()
+    others = len(peers)
+    prob_all = pltpu.make_async_remote_copy(
+        src_ref=heard.at[pl.ds(0, others)], dst_ref=heard.at[pl.ds(0, others)],
+        send_sem=prob_send, recv_sem=prob_recv, device_id={"sub": twin}, device_id_type=MESH,
+    )
+    prob_all.wait_recv()
+    prob_all.wait_send()
     core_in(1, 3)
 
     back = lax.dot_general(
@@ -207,9 +209,10 @@
     )
     both = jnp.concatenate([pre[0], pre[1], pre[2]], axis=1)
     gate, up = both[:, :units], both[:, units:]
-    front_all = tok[:, :, pl.ds(0, LANES)].reshape(count * SLOT, LANES).astype(jnp.float32)
-    lane_all = lax.broadcasted_iota(jnp.int32, front_all.shape, 1)
-    scale = jnp.sum(jnp.where(lane_all == z, front_all, 0.0), axis=1, keepdims=True)
+    front = jnp.broadcast_to(heard[...], (count, SLOT, LANES)).reshape(count * SLOT, LANES)
+    lane_all = lax.broadcasted_iota(jnp.int32, front.shape, 1)
+    at_row = lane_all == lax.rem(lax.broadcasted_iota(jnp.int32, front.shape, 0), SLOT)
+    scale = jnp.sum(jnp.where(at_row, front, 0.0), axis=1, keepdims=True)
     row = lax.rem(lax.broadcasted_iota(jnp.int32, scale.shape, 0), SLOT)
     scale = jnp.where(row < 12, scale, 0.0)
     own = x * 2 + s
@@ -246,10 +249,7 @@
     for tile in range(units // LANES):
         piece = rounded[:, tile * LANES:(tile + 1) * LANES]
         square = square + piece * piece
-    spread = jnp.where(
-        lane_all == lax.rem(lax.broadcasted_iota(jnp.int32, square.shape, 0), SLOT),
-        jnp.sum(square, axis=1, keepdims=True), 0.0,
-    )
+    spread = jnp.where(at_row, jnp.sum(square, axis=1, keepdims=True), 0.0)
     totals[...] = jnp.sum(spread.reshape(count, SLOT, LANES), axis=1, keepdims=True)
     for plane, column, core in peers:
         pltpu.make_async_remote_copy(
@@ -281,7 +281,6 @@
             sent_all(a, 0, planes + 1)
         sent_all(a, 1, planes)
         sent_all(a, 2, 2 * planes)
-    others = len(peers)
     every = pltpu.make_async_remote_copy(
         src_ref=totals.at[pl.ds(0, others)], dst_ref=returned.at[pl.ds(0, others)],
         send_sem=tot_send, recv_sem=tot_recv, device_id={"sub": twin}, device_id_type=MESH,
@@ -358,14 +357,16 @@
             pltpu.VMEM((tok_rows, width), jnp.bfloat16),
             pltpu.VMEM((picks, tok_rows), jnp.int32),
             pltpu.VMEM((picks, tok_rows), jnp.bfloat16),
-            pltpu.VMEM((count, SLOT, LANES + width), jnp.bfloat16),
+            pltpu.VMEM((count, SLOT, width), jnp.bfloat16),
             pltpu.VMEM((count, SLOT, width), jnp.bfloat16),
             pltpu.VMEM((2 * units, width), jnp.bfloat16),
             pltpu.VMEM((units, width), jnp.bfloat16),
             pltpu.VMEM((3, count * SLOT, 2 * units // 3), jnp.float32),
             pltpu.VMEM((count, 1, LANES), jnp.float32),
+            pltpu.VMEM((planes, 1, LANES), jnp.float32),
+            pltpu.VMEM((count, 1, LANES), jnp.float32),
             dma((7,)), dma((2, 3)), dma((2, count)),
-            dma((2, 3)), dma((2, 4)), dma, dma,
+            dma((2, 3)), dma((2, 4)), dma, dma, dma, dma,
         ],
         compiler_params=pltpu.CompilerParams(
             collective_id=0, has_side_effects=True, vmem_limit_bytes=60 * 1024 * 1024

time: 38.3 us -> 38 us (level)
  no operation moved by 1% of the time
where the time goes in v5:
time: 38 us; the launch traced here: 37.9 us
  Pallas kernels  37.2 us (98%)
  between operations  0.67 us (2%)
    pallas_call x1, Pallas kernels, fused(): pl.pallas_call(functools.partial(gather_kernel, planes=planes), out_shape...  34.9 us
    pallas_call x1, Pallas kernels, fused(): pl.pallas_call(functools.partial(fisher_kernel, planes=planes), out_shape...  2.3 us

profile of v5, /device:TPU:0, one launch (start us, length us, event | category | flops | bytes accessed | tf_op | source)
XLA Modules:
  0.0 37.9 jit_solution(1786585327853103850)
XLA Ops:
  0.6 0.0 copy-start
  0.6 0.0 copy-start.1
  0.7 34.9 %gather_grads.1 = (bf16[4,192,384]{2,1,0:T(8,128)(2,1)S(1)}, f32[16,1,128]{2,1,0:T(1,128)S(1)}) custom-call(bf16[12,4096]{1,0:T(8,128)(2,1)} %tokens.1, bf16[12,4096]{1,0:T(8,128)(2,1)} %cotangent.1, s32[2,12]{1,0:T(2,128)} %bitcast.3, bf16[2,12]{1,0:T(2,128)(2,1)} %bitcast.5, bf16[1,384,4096]{2,1,0:T(8,128)(2,1)} %w_gate.1, bf16[1,384,4096]{2,1,0:T(8,128)(2,1)} %w_up.1, ...), custom_call_target="tpu_custom_call" | custom-call | flops 2000000000 | bytes 12000000 | tf_op jit(solution)/shard_map/gather_grads/pallas_call | solution.py:347
  35.6 0.0 copy-done
  35.6 0.0 copy-done.1
  35.6 2.3 %fisher_masks.1 = (f32[1,384,1536]{2,1,0:T(8,128)}, f32[1,384]{1,0:T(1,128)}, f32[2,12]{1,0:T(2,128)}) custom-call(bf16[4,192,384]{2,1,0:T(8,128)(2,1)S(1)} %get-tuple-element.8.grads, f32[16,1,128]{2,1,0:T(1,128)S(1)} %get-tuple-element.9.returned, s32[2,12]{1,0:T(2,128)S(1)} %bitcast.4, s32[1,1536]{1,0:T(1,128)S(1)} %copy-done.1), custom_call_target="tpu_custom_call" | custom-call | flops 300000000 | bytes 3000000 | tf_op jit(solution)/shard_map/fisher_masks/pallas_call | solution.py:377
Async XLA Ops:
  0.6 34.9 %copy-start = (s32[12,2]{0,1:T(2,128)S(1)}, s32[12,2]{0,1:T(2,128)}, u32[]{:S(2)}) copy-start(s32[12,2]{0,1:T(2,128)} %param.10) | copy-start | bytes 292
  0.6 34.9 %copy-start.1 = (s32[1,1536]{1,0:T(1,128)S(1)}, s32[1,1536]{1,0:T(1,128)}, u32[]{:S(2)}) copy-start(s32[1,1536]{1,0:T(1,128)} %keep.1) | copy-start | bytes 18436
